TPU v7x, 32 devices: a whole 2x2x4 slice. The times are simulated.
32 devices in a mesh: kpt: 2 (over y), row: 4 (over z), col: 2 (over x), rep: 2 (over core).
Axes of the slice: x: 2, y: 2, z: 4, core: 2. Of those that a mesh axis runs over, the one named last changes fastest.
Arguments:
- hamiltonian: bfloat16 [256, 6, 128, 128], P(('kpt', 'row'), 'rep'), parts along dimension 0, may hold values from -0.21875 to 0.21875
- pattern: int32 [128, 6], P('row', 'rep'), may hold values from 0 to 127, as said below
- vectors: bfloat16 [256, 32768], P('col', ('kpt', 'row')), parts along dimension 1, may hold values from -6 to 6
- spectrum: float32 [4], P('kpt'), parts along dimension 0, may hold values from 0.5 to 1.5
Outputs:
- filtered: bfloat16 [256, 32768], P('col', ('kpt', 'row')), parts along dimension 1
- gram: float32 [512, 256], P(('kpt', 'row'), 'col'), parts along dimension 0
There are 2 independent parts, one for each index of `kpt`. A program takes and returns all parts, laid end to end along the dimension named above; an argument that names none is the same for every part. Nothing has to cross between parts.
Inputs may be any that keep to these rules, and one draw needn't show every extreme that they name: Each block row i names 6 different blocks; pattern[i, 0] = i, pattern[i, 1] = (i - 1) mod 128, pattern[i, 2] = (i + 1) mod 128, and every entry is (i + o) mod 128 with |o| <= 63.
All inputs are finite; a program needn't handle non-finite values.
Results may differ from a plain program's by a relative error of at most 0.0085.
Values may be sent and summed in bfloat16 or wider, within the bound.
A program may use at most 64 MiB of HBM per device.

v0:
```python
import jax
import jax.numpy as jnp
from jax import lax
from jax.sharding import PartitionSpec as P


def shifted(value, axis, steps):
    count = lax.axis_size(axis)
    pairs = [(source, (source + steps) % count) for source in range(count)]
    return lax.ppermute(value, axis, pairs)


def on_device(hamiltonian, pattern, vectors, spectrum):
    row_blocks = hamiltonian.shape[0]
    width = hamiltonian.shape[2]
    per_dev = vectors.shape[0]
    local_rows = vectors.shape[1]
    row_count = lax.axis_size("row")
    total_blocks = row_blocks * row_count
    total_rows = local_rows * row_count
    here = lax.axis_index("row")
    global_rows = here * row_blocks + jnp.arange(row_blocks, dtype=jnp.int32)
    offsets = (
        pattern - global_rows[:, None] + total_blocks // 2
    ) % total_blocks - total_blocks // 2
    window_index = offsets + jnp.arange(row_blocks, dtype=jnp.int32)[:, None] + 2 * row_blocks
    centre = spectrum[0]
    half_width = spectrum[1]

    def product_terms(slab):
        received = {}
        for step_by in (2, 1, -1, -2):
            received[step_by] = shifted(slab, "row", step_by)
        window = jnp.concatenate(
            [received[2], received[1], slab, received[-1], received[-2]], axis=1
        )
        blocks = window.reshape(per_dev, 5 * row_blocks, width)
        picked = jnp.take(blocks, window_index, axis=1)
        terms = jnp.einsum(
            "kisc,isrc->kir", picked, hamiltonian, preferred_element_type=jnp.float32
        )
        return terms.reshape(per_dev, local_rows)

    def filter_step(slab, factor, previous):
        terms = product_terms(slab)
        summed = lax.psum(terms, "rep")
        result = factor * (summed - centre * slab.astype(jnp.float32)) / half_width
        if previous is not None:
            result = result - previous.astype(jnp.float32)
        return result.astype(jnp.bfloat16)

    first = filter_step(vectors, 1.0, None)
    filtered = filter_step(first, 2.0, vectors)
    every_vector = lax.all_gather(filtered, "col", axis=0, tiled=True)
    gram = (
        lax.psum_scatter(
            lax.dot_general(
                every_vector, filtered, (((1,), (1,)), ((), ())), preferred_element_type=jnp.float32
            ).astype(jnp.bfloat16),
            "row",
            scatter_dimension=0,
            tiled=True,
        ).astype(jnp.float32)
        / total_rows
    )
    return (filtered, gram)


def solution(mesh):
    in_specs = (
        P(("kpt", "row"), "rep", None, None),
        P("row", "rep"),
        P("col", ("kpt", "row")),
        P("kpt"),
    )
    out_specs = (P("col", ("kpt", "row")), P(("kpt", "row"), "col"))
    return jax.shard_map(
        on_device, mesh=mesh, in_specs=in_specs, out_specs=out_specs, check_vma=False
    )
```

profile of v0, /device:TPU:0, one launch (start us, length us, event | category | flops | bytes accessed | tf_op | source)
XLA Modules:
  0.0 363.0 jit_solution(16908792636185628837)
XLA Ops:
  7.2 2.4 copy.22
  9.6 4.0 %collective-permute-start = (bf16[128,4096]{0,1:T(8,128)(2,1)}, bf16[128,4096]{0,1:T(8,128)(2,1)}, u32[]{:S(2)}, u32[]{:S(2)}) collective-permute-start(bf16[128,4096]{0,1:T(8,128)(2,1)} %copy.22), channel_id=1, source_target_pairs={{0,8},{4,12},{8,0},{12,4},{1,9},{5,13},{9,1},{13,5},{2,10},{6,14},... | collective-permute-start | bytes 3145736 | tf_op jit(solution)/shard_map/ppermute | solution.py:10
  13.7 1.6 collective-permute-start.1
  15.3 2.2 collective-permute-start.2
  18.5 64.4 %collective-permute-done = bf16[128,4096]{0,1:T(8,128)(2,1)} collective-permute-done((bf16[128,4096]{0,1:T(8,128)(2,1)}, bf16[128,4096]{0,1:T(8,128)(2,1)}, u32[]{:S(2)}, u32[]{:S(2)}) %collective-permute-start) | collective-permute-done | bytes 1048608 | tf_op jit(solution)/shard_map/ppermute | solution.py:10
  83.0 2.3 constant_dynamic-update-slice_fusion.4
  85.2 2.3 constant_dynamic-update-slice_fusion.3
  88.6 2.3 constant_dynamic-update-slice_fusion.1
  90.9 2.3 constant_dynamic-update-slice_fusion
  93.1 8.0 %copy.27 = bf16[128,160,128]{2,0,1:T(8,128)(2,1)} copy(bf16[128,160,128]{0,2,1:T(8,128)(2,1)} %bitcast) | data formatting | bytes 10485760 | tf_op jit(solution)/shard_map/reshape | solution.py:37
  101.1 5.2 %gather_fusion = bf16[96,128,128]{2,1,0:T(8,128)(2,1)} fusion(bf16[128,160,128]{2,0,1:T(8,128)(2,1)} %copy.27, s32[1024]{0:T(1024)S(1)} %pad_clamp_fusion), kind=kCustom, calls=%fused_computation.clone | custom fusion | bytes 6291840 | tf_op jit(solution)/shard_map/jit(_take)/gather | solution.py:38
  106.3 4.8 %fusion.2 = f32[32,128,128,1]{1,2,3,0:T(8,128)} fusion(bf16[32,3,128,128]{3,2,1,0:T(8,128)(2,1)S(1)} %copy-done, bf16[32,3,128,128]{3,2,1,0:T(8,128)(2,1)} %bitcast.29, pred[32,3]{1,0:T(8,128)(4,1)S(1)} %copy.20), kind=kOutput, calls=%fused_computation.4 | convolution fusion | flops 404226048 | bytes 8388704 | tf_op jit(solution)/shard_map/kisc,isrc->kir/dot_general | solution.py:39
  111.8 40.3 %all-reduce.3.cloned.1.call-done = f32[128,4096]{0,1:T(8,128)} async-done(((f32[128,4096]{0,1:T(8,128)}), f32[128,4096]{0,1:T(8,128)}) %all-reduce.3.cloned.1.call-update) | async-done | bytes 2097168 | tf_op jit(solution)/shard_map/psum | solution.py:46
  152.1 3.5 fusion.10
  155.6 2.7 collective-permute-start.3
  158.3 1.5 collective-permute-start.4
  159.8 2.3 collective-permute-start.5
  162.1 65.4 %collective-permute-done.3 = bf16[128,4096]{0,1:T(8,128)(2,1)S(1)} collective-permute-done((bf16[128,4096]{0,1:T(8,128)(2,1)S(1)}, bf16[128,4096]{0,1:T(8,128)(2,1)S(1)}, u32[]{:S(2)}, u32[]{:S(2)}) %collective-permute-start.3) | collective-permute-done | bytes 1048608 | tf_op jit(solution)/shard_map/ppermute | solution.py:10
  227.5 1.1 constant_dynamic-update-slice_fusion.9
  228.6 1.1 constant_dynamic-update-slice_fusion.8
  229.6 1.1 constant_dynamic-update-slice_fusion.7
  230.7 1.1 constant_dynamic-update-slice_fusion.6
  232.9 8.1 %copy.30 = bf16[128,160,128]{2,0,1:T(8,128)(2,1)} copy(bf16[128,160,128]{0,2,1:T(8,128)(2,1)} %bitcast.9) | data formatting | bytes 10485760 | tf_op jit(solution)/shard_map/reshape | solution.py:37
  241.0 5.2 %gather_fusion.1 = bf16[96,128,128]{2,1,0:T(8,128)(2,1)} fusion(bf16[128,160,128]{2,0,1:T(8,128)(2,1)} %copy.30, s32[1024]{0:T(1024)S(1)} %pad_clamp_fusion), kind=kCustom, calls=%fused_computation.1.clone | custom fusion | bytes 6291840 | tf_op jit(solution)/shard_map/jit(_take)/gather | solution.py:38
  246.2 4.7 %fusion = f32[32,128,128,1]{1,2,3,0:T(8,128)} fusion(bf16[32,3,128,128]{3,2,1,0:T(8,128)(2,1)S(1)} %copy-done, bf16[32,3,128,128]{3,2,1,0:T(8,128)(2,1)} %bitcast.28, pred[32,3]{1,0:T(8,128)(4,1)S(1)} %copy.20), kind=kOutput, calls=%fused_computation.2 | convolution fusion | flops 404226048 | bytes 8388704 | tf_op jit(solution)/shard_map/kisc,isrc->kir/dot_general | solution.py:39
  251.0 42.3 %all-reduce.5.cloned.1.call-done = f32[128,4096]{0,1:T(8,128)} async-done(((f32[128,4096]{0,1:T(8,128)}), f32[128,4096]{0,1:T(8,128)}) %all-reduce.5.cloned.1.call-update) | async-done | bytes 2097168 | tf_op jit(solution)/shard_map/psum | solution.py:46
  293.3 5.0 %fusion.11 = bf16[128,4096]{0,1:T(8,128)(2,1)} fusion(bf16[128,4096]{0,1:T(8,128)(2,1)} %copy.22, f32[128,4096]{0,1:T(8,128)} %all-reduce.5.cloned.1.call-done, bf16[128,4096]{0,1:T(8,128)(2,1)} %copy-done.2, f32[]{:T(128)} %bitcast.8, f32[]{:T(128)} %bitcast.7), kind=kLoop, calls=%fused_computation.15 | loop fusion | flops 4194304 | bytes 5242888 | tf_op jit(solution)/shard_map/convert_element_type | solution.py:50
  298.3 34.4 %all-gather.2.cloned.1.call-done = bf16[256,4096]{0,1:T(8,128)(2,1)} async-done(((bf16[128,4096]{0,1:T(8,128)(2,1)}), bf16[256,4096]{0,1:T(8,128)(2,1)}) %all-gather.2.cloned.1.call-update) | async-done | bytes 2097168 | tf_op jit(solution)/shard_map/all_gather | solution.py:54
  332.7 3.2 convolution_convert_fusion
  335.9 2.3 copy.31
  338.2 16.9 %reduce-scatter.2.cloned.1.call-done = bf16[64,128]{1,0:T(8,128)(2,1)} async-done(((bf16[256,128]{1,0:T(8,128)(2,1)}), bf16[64,128]{1,0:T(8,128)(2,1)}) %reduce-scatter.2.cloned.1.call-update) | async-done | bytes 16400 | tf_op jit(solution)/shard_map/reduce_scatter | solution.py:56
  355.1 1.3 convert_multiply_fusion.1
  (29 shorter events, 4.0 us)
Async XLA Ops:
  7.2 99.1 %copy-start = (bf16[32,3,128,128]{3,2,1,0:T(8,128)(2,1)S(1)}, bf16[32,3,128,128]{3,2,1,0:T(8,128)(2,1)}, u32[]{:S(2)}) copy-start(bf16[32,3,128,128]{3,2,1,0:T(8,128)(2,1)} %param.6) | copy-start | bytes 9437188
  7.2 144.9 %all-reduce.3.cloned.1.call-start = ((), (), s32[]{:S(2)}) async-start(), calls=%async_computation.1 | async-start | bytes 4194304 | tf_op jit(solution)/shard_map/psum | solution.py:46
  9.6 73.3 %collective-permute-start = (bf16[128,4096]{0,1:T(8,128)(2,1)}, bf16[128,4096]{0,1:T(8,128)(2,1)}, u32[]{:S(2)}, u32[]{:S(2)}) collective-permute-start(bf16[128,4096]{0,1:T(8,128)(2,1)} %copy.22), channel_id=1, source_target_pairs={{0,8},{4,12},{8,0},{12,4},{1,9},{5,13},{9,1},{13,5},{2,10},{6,14},... | collective-permute-start | bytes 3145736 | tf_op jit(solution)/shard_map/ppermute | solution.py:10
  13.7 71.6 %collective-permute-start.1 = (bf16[128,4096]{0,1:T(8,128)(2,1)}, bf16[128,4096]{0,1:T(8,128)(2,1)}, u32[]{:S(2)}, u32[]{:S(2)}) collective-permute-start(bf16[128,4096]{0,1:T(8,128)(2,1)} %copy.22), channel_id=1, source_target_pairs={{0,4},{4,8},{8,12},{12,0},{1,5},{5,9},{9,13},{13,1},{2,6},{6,10},{... | collective-permute-start | bytes 3145736 | tf_op jit(solution)/shard_map/ppermute | solution.py:10
  15.3 73.3 %collective-permute-start.2 = (bf16[128,4096]{0,1:T(8,128)(2,1)}, bf16[128,4096]{0,1:T(8,128)(2,1)}, u32[]{:S(2)}, u32[]{:S(2)}) collective-permute-start(bf16[128,4096]{0,1:T(8,128)(2,1)} %copy.22), channel_id=1, source_target_pairs={{0,12},{4,0},{8,4},{12,8},{1,13},{5,1},{9,5},{13,9},{2,14},{6,2},{... | collective-permute-start | bytes 3145736 | tf_op jit(solution)/shard_map/ppermute | solution.py:10
  18.5 69.0 %copy-start.1 = (bf16[128,4096]{0,1:T(8,128)(2,1)S(1)}, bf16[128,4096]{0,1:T(8,128)(2,1)}, u32[]{:S(2)}) copy-start(bf16[128,4096]{0,1:T(8,128)(2,1)} %copy.22) | copy-start | bytes 3145732
  106.3 4.8 %copy-start.3 = (f32[2]{0:T(128)S(1)}, f32[2]{0:T(128)}, u32[]{:S(2)}) copy-start(f32[2]{0:T(128)} %param.9) | copy-start | bytes 28
  111.1 182.2 %all-reduce.5.cloned.1.call-start = ((), (), s32[]{:S(2)}) async-start(), calls=%async_computation.2 | async-start | bytes 4194304 | tf_op jit(solution)/shard_map/psum | solution.py:46
  155.5 75.2 %copy-start.2 = (bf16[128,4096]{0,1:T(8,128)(2,1)}, bf16[128,4096]{0,1:T(8,128)(2,1)S(1)}, u32[]{:S(2)}) copy-start(bf16[128,4096]{0,1:T(8,128)(2,1)S(1)} %fusion.10) | copy-start | bytes 3145732
  155.6 71.9 %collective-permute-start.3 = (bf16[128,4096]{0,1:T(8,128)(2,1)S(1)}, bf16[128,4096]{0,1:T(8,128)(2,1)S(1)}, u32[]{:S(2)}, u32[]{:S(2)}) collective-permute-start(bf16[128,4096]{0,1:T(8,128)(2,1)S(1)} %fusion.10), channel_id=1, source_target_pairs={{0,8},{4,12},{8,0},{12,4},{1,9},{5,13},{9,1},{13,5},{2,10},{6,14},... | collective-permute-start | bytes 3145736 | tf_op jit(solution)/shard_map/ppermute | solution.py:10
  158.3 70.3 %collective-permute-start.4 = (bf16[128,4096]{0,1:T(8,128)(2,1)S(1)}, bf16[128,4096]{0,1:T(8,128)(2,1)S(1)}, u32[]{:S(2)}, u32[]{:S(2)}) collective-permute-start(bf16[128,4096]{0,1:T(8,128)(2,1)S(1)} %fusion.10), channel_id=1, source_target_pairs={{0,4},{4,8},{8,12},{12,0},{1,5},{5,9},{9,13},{13,1},{2,6},{6,10},{... | collective-permute-start | bytes 3145736 | tf_op jit(solution)/shard_map/ppermute | solution.py:10
  159.8 70.9 %collective-permute-start.5 = (bf16[128,4096]{0,1:T(8,128)(2,1)S(1)}, bf16[128,4096]{0,1:T(8,128)(2,1)S(1)}, u32[]{:S(2)}, u32[]{:S(2)}) collective-permute-start(bf16[128,4096]{0,1:T(8,128)(2,1)S(1)} %fusion.10), channel_id=1, source_target_pairs={{0,12},{4,0},{8,4},{12,8},{1,13},{5,1},{9,5},{13,9},{2,14},{6,2},{... | collective-permute-start | bytes 3145736 | tf_op jit(solution)/shard_map/ppermute | solution.py:10
  250.9 81.7 %all-gather.2.cloned.1.call-start = ((), (), s32[]{:S(2)}) async-start(), calls=%async_computation.3 | async-start | bytes 3145728 | tf_op jit(solution)/shard_map/all_gather | solution.py:54
  298.3 56.9 %reduce-scatter.2.cloned.1.call-start = ((), (), s32[]{:S(2)}) async-start(), calls=%async_computation.4 | async-start | bytes 81920 | tf_op jit(solution)/shard_map/reduce_scatter | solution.py:56
Sparse Core Ops, SparseCore 0:
  111.2 40.8 all-reduce.2
  251.1 42.1 all-reduce.4
  298.4 34.2 all-gather.1
  336.0 19.0 reduce-scatter.1
where the time goes:
time: 364 us; the launch traced here: 363 us
  waiting for transfers between devices  264 us (73%)
  local copies, waits for them, and re-layouts  47.7 us (13%)
  starting transfers between devices  14.6 us (4%)
  between operations  13.8 us (4%)
  matrix products  12.7 us (3%)
  other arithmetic  10.5 us (3%)
    ppermute x6, waiting for transfers between devices, shifted(): return lax.ppermute(value, axis, pairs)  130 us
    psum x2, waiting for transfers between devices, filter_step(): summed = lax.psum(terms, 'rep')  82.6 us
    all_gather x1, waiting for transfers between devices, on_device(): every_vector = lax.all_gather(filtered, 'col', axis=0, tiled=True)  34.4 us
    unnamed x18, local copies, waits for them, and re-layouts  17 us
    reduce_scatter x1, waiting for transfers between devices, on_device(): lax.psum_scatter(lax.dot_general(every_vector, filtered, (((1,), (1,)), (...  16.9 us
    reshape x2, local copies, waits for them, and re-layouts, product_terms(): blocks = window.reshape(per_dev, 5 * row_blocks, width)  16.1 us
    ppermute x6, starting transfers between devices, shifted(): return lax.ppermute(value, axis, pairs)  14.4 us
    gather x2, local copies, waits for them, and re-layouts, product_terms(): picked = jnp.take(blocks, window_index, axis=1)  10.4 us
  transfers between devices with their start and end apart: 10, of which 6 were waited for; matrix products, arithmetic and copies ran while one was open for 4% of the time, Pallas kernels for 0%

commit v1 on v0

v1 whole, which is shorter than its diff:
```python
import functools

import jax
import jax.numpy as jnp
from jax import lax
from jax.experimental import pallas as pl
from jax.experimental.pallas import tpu as pltpu
from jax.sharding import PartitionSpec as P

MESH = pl.DeviceIdType.MESH
NT = (((1,), (1,)), ((), ()))
CHUNKS = 2
UNROLL = 4


def kernel(
    R, C, hops, line, h_ref, pat_ref, vec_ref, spec_ref, out_ref, gram_ref,
    hall, pvm, psm, stage, filt, gbuf, part, recv_a, send_b, recv_b, *rest,
):
    wins = rest[: 2 * CHUNKS]
    (z_send, z_recv, h_send, h_recv, p_send, p_recv, loc, o_send, o_recv,
     g_send, g_recv, a_send, a_recv, b_send, b_recv) = rest[2 * CHUNKS:]
    win1, win2 = wins[:CHUNKS], wins[CHUNKS:]
    k, r, c, p = (lax.axis_index(n) for n in ("kpt", "row", "col", "rep"))
    G = 2 * C
    g = c * 2 + p
    nb, half_nnz = h_ref.shape[0], h_ref.shape[1]
    B = h_ref.shape[2]
    V = stage.shape[0]
    vc = V // CHUNKS
    bw = gbuf.shape[1]
    ct = part.shape[3]
    rt = send_b.shape[1]
    other = 1 - p

    local_v = pltpu.make_async_copy(vec_ref.at[pl.ds(pl.multiple_of(p * V, V), V)], stage, loc.at[0])
    local_v.start()
    local_h = pltpu.make_async_copy(h_ref, hall.at[p], loc.at[1])
    local_h.start()
    local_p = pltpu.make_async_copy(pat_ref, psm.at[p], loc.at[2])
    local_p.start()

    barrier = pltpu.get_barrier_semaphore()
    for j in range(1, 2 * R):
        o = lax.rem(r * 2 + p + j, 2 * R)
        pl.semaphore_signal(barrier, inc=1, device_id=(k, o // 2, c, lax.rem(o, 2)), device_id_type=MESH)
    for j in range(1, C):
        o = lax.rem(c + j, C)
        for q in range(2):
            pl.semaphore_signal(barrier, inc=1, device_id=(k, r, o, q), device_id_type=MESH)

    def slot(d):
        return r + d if line else 2 + d

    local_v.wait()
    own = slot(0) * nb

    def block_major(i, _):
        for q in range(CHUNKS):
            win1[q][own + i] = stage[pl.ds(q * vc, vc), pl.ds(pl.multiple_of(i * B, B), B)]
        return 0

    lax.fori_loop(0, nb, block_major, 0)
    pl.semaphore_wait(barrier, 2 * R - 1 + 2 * (C - 1))

    def z_copy(step, q, way, h):
        win = (win1, win2)[step][q]
        sign = -1 if way == 0 else 1
        src = slot(sign * h)
        dst = src if line else slot(sign * (h + 1))
        target = r + 1 if way == 0 else r - 1
        target = lax.rem(target + R, R)
        return pltpu.make_async_remote_copy(
            src_ref=win.at[pl.ds(src * nb, nb)],
            dst_ref=win.at[pl.ds(dst * nb, nb)],
            send_sem=z_send.at[step, q, way, h],
            recv_sem=z_recv.at[step, q, way, h],
            device_id=(k, target, c, p),
            device_id_type=MESH,
        )

    def z_arrival(step, q, way, h):
        win = (win1, win2)[step][q]
        sign = -1 if way == 0 else 1
        dst = slot(sign * (h + 1))
        target = lax.rem((r - 1 if way == 0 else r + 1) + R, R)
        return pltpu.make_async_remote_copy(
            src_ref=win.at[pl.ds(dst * nb, nb)],
            dst_ref=win.at[pl.ds(dst * nb, nb)],
            send_sem=z_send.at[step, q, way, h],
            recv_sem=z_recv.at[step, q, way, h],
            device_id=(k, target, c, p),
            device_id_type=MESH,
        )

    def when(cond, fn):
        if line:
            pl.when(cond)(fn)
        else:
            fn()

    def sends(way, h):
        if way == 0:
            return jnp.logical_and(r + 1 < R, r - h >= 0)
        return jnp.logical_and(r - 1 >= 0, r + h < R)

    def receives(way, h):
        return r - 1 - h >= 0 if way == 0 else r + 1 + h < R

    def z_start(step, q, h):
        for way in range(2):
            when(sends(way, h), lambda way=way: z_copy(step, q, way, h).start())

    def z_wait(step, q, h):
        for way in range(2):
            when(receives(way, h), lambda way=way: z_arrival(step, q, way, h).wait_recv())

    def z_forward(step, q, h):
        for way in range(2):
            when(receives(way, h - 1), lambda way=way: z_arrival(step, q, way, h - 1).wait_recv())
            when(sends(way, h), lambda way=way: z_copy(step, q, way, h).start())

    partner = (k, r, c, other)
    for q in range(CHUNKS):
        z_start(0, q, 0)
    send_p = pltpu.make_async_remote_copy(pat_ref, pvm, p_send, p_recv, device_id=partner, device_id_type=MESH)
    send_p.start()
    send_h = pltpu.make_async_remote_copy(h_ref, hall.at[p], h_send, h_recv, device_id=partner, device_id_type=MESH)
    send_h.start()
    arrive_h = pltpu.make_async_remote_copy(h_ref, hall.at[other], h_send, h_recv, device_id=partner, device_id_type=MESH)
    send_p.wait_recv()
    other_p = pltpu.make_async_copy(pvm, psm.at[other], loc.at[3])
    other_p.start()

    for h in range(1, hops):
        for q in range(CHUNKS):
            z_forward(0, q, h)

    local_h.wait()
    local_p.wait()
    other_p.wait()
    arrive_h.wait_recv()

    centre = spec_ref[0]
    inverse = 1.0 / jnp.full((vc, B), spec_ref[1], jnp.float32)
    total = nb * R

    def index(half, i, s):
        named = psm[half, i, s]
        if line:
            return named
        return lax.rem(named - (r - 2) * nb + total, total)

    def product(win, i):
        sums = None
        for half in range(2):
            for s in range(half_nnz):
                term = lax.dot_general(
                    win[index(half, i, s)], hall[half, i, s], NT, preferred_element_type=jnp.float32
                )
                sums = term if sums is None else sums + term
        return sums

    for q in range(CHUNKS):
        z_wait(0, q, hops - 1)

        def first_row(i, _, q=q):
            start = win1[q][own + i].astype(jnp.float32)
            win2[q][own + i] = ((product(win1[q], i) - centre * start) * inverse).astype(jnp.bfloat16)
            return 0

        lax.fori_loop(0, nb, first_row, 0, unroll=UNROLL)
        z_start(1, q, 0)

    for h in range(1, hops):
        for q in range(CHUNKS):
            z_forward(1, q, h)

    def group(j):
        o = lax.rem(g + j, G)
        return o, (k, r, o // 2, lax.rem(o, 2))

    def vec_row(gi, q):
        return pl.ds(pl.multiple_of(gi * V + q * vc, vc), vc)

    tail = []
    for q in range(CHUNKS):
        z_wait(1, q, hops - 1)

        def filtered_row(i, _, q=q):
            first = win2[q][own + i].astype(jnp.float32)
            start = win1[q][own + i].astype(jnp.float32)
            value = 2.0 * ((product(win2[q], i) - centre * first) * inverse) - start
            filt[pl.ds(q * vc, vc), pl.ds(pl.multiple_of(i * B, B), B)] = value.astype(jnp.bfloat16)
            return 0

        lax.fori_loop(0, nb, filtered_row, 0, unroll=UNROLL)
        for j in range(1, G):
            o, device = group(j)
            copy = pltpu.make_async_remote_copy(
                filt.at[pl.ds(q * vc, vc), pl.ds(pl.multiple_of(o * bw, bw), bw)],
                gbuf.at[vec_row(g, q)],
                g_send.at[q, j], g_recv.at[q, j], device_id=device, device_id_type=MESH,
            )
            copy.start()
            tail.append(copy)
        gbuf[vec_row(g, q), :] = filt[pl.ds(q * vc, vc), pl.ds(pl.multiple_of(g * bw, bw), bw)]
        rows = pl.ds(pl.multiple_of(p * V + q * vc, vc), vc)
        keep = pltpu.make_async_copy(filt.at[pl.ds(q * vc, vc)], out_ref.at[rows], loc.at[4 + q])
        keep.start()
        copy = pltpu.make_async_remote_copy(
            filt.at[pl.ds(q * vc, vc)], out_ref.at[rows], o_send.at[q], o_recv.at[q],
            device_id=partner, device_id_type=MESH,
        )
        copy.start()
        tail.append(copy)

    for q in range(CHUNKS):
        for j in range(1, G):
            source = lax.rem(g - j + G, G)
            pltpu.make_async_remote_copy(
                gbuf.at[vec_row(source, q)], gbuf.at[vec_row(source, q)],
                g_send.at[q, j], g_recv.at[q, j], device_id=group(j)[1], device_id_type=MESH,
            ).wait_recv()

    everything = gbuf[...]
    for cc in range(C):
        tile = lax.dot_general(
            everything, gbuf[pl.ds(cc * ct, ct), :], NT, preferred_element_type=jnp.float32
        ).astype(jnp.bfloat16)
        part[cc, 0] = tile[: rt * R // 2]
        part[cc, 1] = tile[rt * R // 2:]
    for j in range(1, G):
        o, device = group(j)
        copy = pltpu.make_async_remote_copy(
            part.at[o // 2, lax.rem(o, 2)], recv_a.at[g], a_send.at[j], a_recv.at[j],
            device_id=device, device_id_type=MESH,
        )
        copy.start()
        tail.append(copy)
    recv_a[g] = part[c, p]
    for j in range(1, G):
        source = lax.rem(g - j + G, G)
        pltpu.make_async_remote_copy(
            recv_a.at[source], recv_a.at[source], a_send.at[j], a_recv.at[j],
            device_id=group(j)[1], device_id_type=MESH,
        ).wait_recv()
    summed = recv_a[0].astype(jnp.float32)
    for j in range(1, G):
        summed = summed + recv_a[j].astype(jnp.float32)
    for j in range(R // 2):
        send_b[j] = summed[j * rt:(j + 1) * rt].astype(send_b.dtype)

    def b_copy(j, q):
        return pltpu.make_async_remote_copy(
            send_b.at[j], recv_b.at[r], b_send.at[j, q], b_recv.at[r],
            device_id=(k, p * (R // 2) + j, c, q), device_id_type=MESH,
        )

    def b_elsewhere(j, q):
        return jnp.logical_or(r != p * (R // 2) + j, p != q)

    for j in range(R // 2):
        for q in range(2):
            pl.when(b_elsewhere(j, q))(lambda j=j, q=q: b_copy(j, q).start())
        pl.when(r == p * (R // 2) + j)(lambda j=j: recv_b.__setitem__(r, send_b[j]))
    mine = r // (R // 2)
    for source in range(R):
        arrive = pltpu.make_async_remote_copy(
            recv_b.at[source], recv_b.at[source], b_send.at[0, 0], b_recv.at[source],
            device_id=(k, source, c, mine), device_id_type=MESH,
        )
        pl.when(jnp.logical_or(r != source, p != mine))(lambda arrive=arrive: arrive.wait_recv())
    gram = recv_b[0].astype(jnp.float32)
    for source in range(1, R):
        gram = gram + recv_b[source].astype(jnp.float32)
    gram_ref[...] = gram * (1.0 / (total * B))

    for step in range(2):
        for q in range(CHUNKS):
            for h in range(hops):
                for way in range(2):
                    when(sends(way, h), lambda a=(step, q, way, h): z_copy(*a).wait_send())
    send_p.wait_send()
    send_h.wait_send()
    for copy in tail:
        copy.wait_send()
    for j in range(R // 2):
        for q in range(2):
            pl.when(b_elsewhere(j, q))(lambda j=j, q=q: b_copy(j, q).wait_send())
    for q in range(CHUNKS):
        rows = pl.ds(pl.multiple_of(p * V + q * vc, vc), vc)
        pltpu.make_async_copy(filt.at[pl.ds(q * vc, vc)], out_ref.at[rows], loc.at[4 + q]).wait()
        theirs = pl.ds(pl.multiple_of(other * V + q * vc, vc), vc)
        pltpu.make_async_remote_copy(
            filt.at[pl.ds(q * vc, vc)], out_ref.at[theirs], o_send.at[q], o_recv.at[q],
            device_id=partner, device_id_type=MESH,
        ).wait_recv()


def on_device(R, C, hamiltonian, pattern, vectors, spectrum):
    nb, half_nnz, B, _ = hamiltonian.shape
    per_dev, local_rows = vectors.shape
    line = R <= 4
    hops = R - 1 if line else 2
    slots = R if line else 5
    V = per_dev // 2
    vc = V // CHUNKS
    G = 2 * C
    K = per_dev * C
    bw = local_rows // G
    rt, ct = K // R, per_dev
    b_type = jnp.bfloat16 if rt % 16 == 0 else jnp.float32
    bf16 = jnp.bfloat16
    dma = pltpu.SemaphoreType.DMA
    return pl.pallas_call(
        functools.partial(kernel, R, C, hops, line),
        out_shape=(
            jax.ShapeDtypeStruct((per_dev, local_rows), bf16),
            jax.ShapeDtypeStruct((rt, ct), jnp.float32),
        ),
        in_specs=[
            pl.BlockSpec(memory_space=pl.ANY),
            pl.BlockSpec(memory_space=pl.ANY),
            pl.BlockSpec(memory_space=pl.ANY),
            pl.BlockSpec(memory_space=pltpu.SMEM),
        ],
        out_specs=(pl.BlockSpec(memory_space=pl.ANY), pl.BlockSpec(memory_space=pltpu.VMEM)),
        scratch_shapes=[
            pltpu.VMEM((2, nb, half_nnz, B, B), bf16),
            pltpu.VMEM((nb, half_nnz), jnp.int32),
            pltpu.SMEM((2, nb, half_nnz), jnp.int32),
            pltpu.VMEM((V, local_rows), bf16),
            pltpu.VMEM((V, local_rows), bf16),
            pltpu.VMEM((K, bw), bf16),
            pltpu.VMEM((C, 2, K // 2, ct), bf16),
            pltpu.VMEM((G, K // 2, ct), bf16),
            pltpu.VMEM((R // 2, rt, ct), b_type),
            pltpu.VMEM((R, rt, ct), b_type),
        ]
        + [pltpu.VMEM((slots * nb, vc, B), bf16)] * (2 * CHUNKS)
        + [
            dma((2, CHUNKS, 2, hops)), dma((2, CHUNKS, 2, hops)),
            dma, dma, dma, dma, dma((4 + CHUNKS,)),
            dma((CHUNKS,)), dma((CHUNKS,)),
            dma((CHUNKS, G)), dma((CHUNKS, G)),
            dma((G,)), dma((G,)),
            dma((R // 2, 2)), dma((R,)),
        ],
        compiler_params=pltpu.CompilerParams(
            collective_id=0, has_side_effects=True, vmem_limit_bytes=40 * 1024 * 1024
        ),
    )(hamiltonian, pattern, vectors, spectrum)


def solution(mesh):
    in_specs = (
        P(("kpt", "row"), "rep", None, None),
        P("row", "rep"),
        P("col", ("kpt", "row")),
        P("kpt"),
    )
    out_specs = (P("col", ("kpt", "row")), P(("kpt", "row"), "col"))
    return jax.shard_map(
        functools.partial(on_device, mesh.shape["row"], mesh.shape["col"]),
        mesh=mesh, in_specs=in_specs, out_specs=out_specs, check_vma=False,
    )
```

time: 364 us -> 97.6 us (0.27)
  waiting for transfers between devices: 264 us -> 0 us
  Pallas kernels: 0 us -> 90.6 us
  local copies, waits for them, and re-layouts: 47.7 us -> 6.12 us
  starting transfers between devices: 14.6 us -> 0 us
  between operations: 13.8 us -> 0.64 us
  matrix products: 12.7 us -> 0 us
  other arithmetic: 10.5 us -> 0 us
    ppermute x6 -> x0, waiting for transfers between devices: 130 us -> none  [shifted(): return lax.ppermute(value, axis, pairs)]
    pallas_call x0 -> x1, Pallas kernels: none -> 90.6 us  [on_device(): pl.pallas_call(functools.partial(kernel, R, C, hops, line), out_shape=(ja...]
    psum x2 -> x0, waiting for transfers between devices: 82.6 us -> none  [filter_step(): summed = lax.psum(terms, 'rep')]
    all_gather x1 -> x0, waiting for transfers between devices: 34.4 us -> none  [on_device(): every_vector = lax.all_gather(filtered, 'col', axis=0, tiled=True)]
    reduce_scatter x1 -> x0, waiting for transfers between devices: 16.9 us -> none  [on_device(): lax.psum_scatter(lax.dot_general(every_vector, filtered, (((1,), (1,)), (...]
    reshape x2 -> x0, local copies, waits for them, and re-layouts: 16.1 us -> none  [product_terms(): blocks = window.reshape(per_dev, 5 * row_blocks, width)]
    ppermute x6 -> x0, starting transfers between devices: 14.4 us -> none  [shifted(): return lax.ppermute(value, axis, pairs)]
    dot_general x3 -> x0, matrix products: 12.7 us -> none  [the longest x2 9.48 us: product_terms(): jnp.einsum('kisc,isrc->kir', picked, hamiltonian, preferred_element_type=...]
  transfers between devices with their start and end apart: 10 -> 0, of which waited for: 6 -> 0; matrix products, arithmetic and copies ran while one was open for 4% -> 0% of each run, Pallas kernels for 0% -> 0%
where the time goes in v1:
time: 97.6 us; the launch traced here: 97.3 us
  Pallas kernels  90.6 us (93%)
  local copies, waits for them, and re-layouts  6.12 us (6%)
    pallas_call x1, Pallas kernels, on_device(): pl.pallas_call(functools.partial(kernel, R, C, hops, line), out_shape=(ja...  90.6 us
    unnamed x9, local copies, waits for them, and re-layouts  6.12 us

profile of v1, /device:TPU:0, one launch (start us, length us, event | category | flops | bytes accessed | tf_op | source)
XLA Modules:
  0.0 97.3 jit_solution(5499126114380531144)
XLA Ops:
  0.6 0.8 copy.6.pat_ref
  1.4 0.0 copy-start
  1.4 1.9 %copy-done = bf16[32,3,128,128]{3,2,1,0:T(8,128)(2,1)S(1)} copy-done((bf16[32,3,128,128]{3,2,1,0:T(8,128)(2,1)S(1)}, bf16[32,3,128,128]{3,2,1,0:T(8,128)(2,1)}, u32[]{:S(2)}) %copy-start) | copy-done | bytes 3145752
  3.3 0.0 copy-start.1
  3.3 1.2 %copy-done.1 = bf16[128,4096]{1,0:T(8,128)(2,1)S(1)} copy-done((bf16[128,4096]{1,0:T(8,128)(2,1)S(1)}, bf16[128,4096]{1,0:T(8,128)(2,1)}, u32[]{:S(2)}) %copy-start.1) | copy-done | bytes 1048600
  4.5 0.0 copy-start.2
  4.5 0.7 copy-done.2
  5.2 90.6 %shard_map.59 = (bf16[128,4096]{1,0:T(8,128)(2,1)S(1)}, f32[64,128]{1,0:T(8,128)S(1)}) custom-call(bf16[32,3,128,128]{3,2,1,0:T(8,128)(2,1)S(1)} %copy-done, s32[32,3]{1,0:T(8,128)S(1)} %copy.6.pat_ref, bf16[128,4096]{1,0:T(8,128)(2,1)S(1)} %copy-done.1, f32[2]{0:T(128)S(1)} %copy-done.2), custom_call_target="tpu_custom_call" | custom-call | tf_op jit(solution)/shard_map/pallas_call | solution.py:316
  95.8 1.0 copy.9
  96.7 0.6 copy.10
Async XLA Ops:
  1.4 1.9 %copy-start = (bf16[32,3,128,128]{3,2,1,0:T(8,128)(2,1)S(1)}, bf16[32,3,128,128]{3,2,1,0:T(8,128)(2,1)}, u32[]{:S(2)}) copy-start(bf16[32,3,128,128]{3,2,1,0:T(8,128)(2,1)} %h_ref.1) | copy-start | bytes 9437188
  3.3 1.2 %copy-start.1 = (bf16[128,4096]{1,0:T(8,128)(2,1)S(1)}, bf16[128,4096]{1,0:T(8,128)(2,1)}, u32[]{:S(2)}) copy-start(bf16[128,4096]{1,0:T(8,128)(2,1)} %vec_ref.1) | copy-start | bytes 3145732
  4.5 0.7 copy-start.2

commit v2 on v1

--- a/solution.py
+++ b/solution.py
@@ -9,25 +9,31 @@
 
 MESH = pl.DeviceIdType.MESH
 NT = (((1,), (1,)), ((), ()))
-CHUNKS = 2
-UNROLL = 4
+NN = (((1,), (0,)), ((), ()))
+UNROLL = 8
 
 
 def kernel(
-    R, C, hops, line, h_ref, pat_ref, vec_ref, spec_ref, out_ref, gram_ref,
+    R, C, hops, line, chunks, h_ref, pat_ref, vec_ref, spec_ref, out_ref, gram_ref,
     hall, pvm, psm, stage, filt, gbuf, part, recv_a, send_b, recv_b, *rest,
 ):
-    wins = rest[: 2 * CHUNKS]
+    wins = rest[: 2 * chunks]
     (z_send, z_recv, h_send, h_recv, p_send, p_recv, loc, o_send, o_recv,
-     g_send, g_recv, a_send, a_recv, b_send, b_recv) = rest[2 * CHUNKS:]
-    win1, win2 = wins[:CHUNKS], wins[CHUNKS:]
+     g_send, g_recv, a_send, a_recv, b_send, b_recv) = rest[2 * chunks:2 * chunks + 15]
+    extra = rest[2 * chunks + 15:]
+    win1, win2 = wins[:chunks], wins[chunks:]
+    ends = bool(extra)
+    if ends:
+        hx, pxv, pxs = extra[:3]
+        s_out, s_in = extra[3:3 + chunks], extra[3 + chunks:3 + 2 * chunks]
+        x_send, x_recv, y_send, y_recv, px_send, px_recv, s_send, s_recv, e_send, e_recv = extra[3 + 2 * chunks:]
     k, r, c, p = (lax.axis_index(n) for n in ("kpt", "row", "col", "rep"))
     G = 2 * C
     g = c * 2 + p
     nb, half_nnz = h_ref.shape[0], h_ref.shape[1]
     B = h_ref.shape[2]
     V = stage.shape[0]
-    vc = V // CHUNKS
+    vc = V // chunks
     bw = gbuf.shape[1]
     ct = part.shape[3]
     rt = send_b.shape[1]
@@ -56,7 +62,7 @@
     own = slot(0) * nb
 
     def block_major(i, _):
-        for q in range(CHUNKS):
+        for q in range(chunks):
             win1[q][own + i] = stage[pl.ds(q * vc, vc), pl.ds(pl.multiple_of(i * B, B), B)]
         return 0
 
@@ -93,47 +99,95 @@
             device_id_type=MESH,
         )
 
+    if ends:
+        outer = jnp.logical_or(r == 0, r == R - 1)
+        inner = jnp.logical_not(outer)
+        low = r < R // 2
+        end = jnp.where(low, 0, R - 1)
+        mate = jnp.where(low, 1 - r, 2 * R - 3 - r)
+        zero_block = nb * R
+        edge_near = jnp.where(low, nb, (R - 1) * nb - 1)
+        edge_far = jnp.where(low, nb * R - 1, 0)
+
     def when(cond, fn):
         if line:
             pl.when(cond)(fn)
         else:
             fn()
 
-    def sends(way, h):
+    def sends(step, way, h):
+        short = 1 if ends and step == 1 else 0
         if way == 0:
-            return jnp.logical_and(r + 1 < R, r - h >= 0)
-        return jnp.logical_and(r - 1 >= 0, r + h < R)
-
-    def receives(way, h):
-        return r - 1 - h >= 0 if way == 0 else r + 1 + h < R
+            return jnp.logical_and(r + 1 < R - short, r - h >= 0)
+        return jnp.logical_and(r - 1 >= short, r + h < R)
+
+    def receives(step, way, h):
+        short = 1 if ends and step == 1 else 0
+        if way == 0:
+            return jnp.logical_and(r < R - short, r - 1 - h >= 0)
+        return jnp.logical_and(r >= short, r + 1 + h < R)
 
     def z_start(step, q, h):
         for way in range(2):
-            when(sends(way, h), lambda way=way: z_copy(step, q, way, h).start())
+            when(sends(step, way, h), lambda way=way: z_copy(step, q, way, h).start())
 
     def z_wait(step, q, h):
         for way in range(2):
-            when(receives(way, h), lambda way=way: z_arrival(step, q, way, h).wait_recv())
+            when(receives(step, way, h), lambda way=way: z_arrival(step, q, way, h).wait_recv())
 
     def z_forward(step, q, h):
         for way in range(2):
-            when(receives(way, h - 1), lambda way=way: z_arrival(step, q, way, h - 1).wait_recv())
-            when(sends(way, h), lambda way=way: z_copy(step, q, way, h).start())
+            when(receives(step, way, h - 1), lambda way=way: z_arrival(step, q, way, h - 1).wait_recv())
+            when(sends(step, way, h), lambda way=way: z_copy(step, q, way, h).start())
 
     partner = (k, r, c, other)
-    for q in range(CHUNKS):
+    for q in range(chunks):
         z_start(0, q, 0)
     send_p = pltpu.make_async_remote_copy(pat_ref, pvm, p_send, p_recv, device_id=partner, device_id_type=MESH)
     send_p.start()
     send_h = pltpu.make_async_remote_copy(h_ref, hall.at[p], h_send, h_recv, device_id=partner, device_id_type=MESH)
     send_h.start()
     arrive_h = pltpu.make_async_remote_copy(h_ref, hall.at[other], h_send, h_recv, device_id=partner, device_id_type=MESH)
+    if ends:
+        piece = nb // 2
+
+        def x_copy(j):
+            part_rows = pl.ds(j * piece, piece)
+            return pltpu.make_async_remote_copy(
+                h_ref.at[part_rows], hx.at[part_rows], x_send.at[j], x_recv.at[j],
+                device_id=(k, mate, c, p), device_id_type=MESH,
+            )
+
+        def y_copy(j):
+            part_rows = pl.ds(j * piece, piece)
+            return pltpu.make_async_remote_copy(
+                hx.at[part_rows], hx.at[part_rows], y_send.at[j], y_recv.at[j],
+                device_id=partner, device_id_type=MESH,
+            )
+
+        def px_copy(q):
+            return pltpu.make_async_remote_copy(
+                pat_ref, pxv, px_send.at[q], px_recv, device_id=(k, mate, c, q), device_id_type=MESH,
+            )
+
+        from_end = jnp.logical_and(outer, p == 1)
+        relay = jnp.logical_and(inner, p == 1)
+        relayed = jnp.logical_and(inner, p == 0)
+
+        @pl.when(from_end)
+        def _():
+            for q in range(2):
+                px_copy(q).start()
+
+        for q in range(chunks):
+            win2[q][zero_block] = jnp.zeros((vc, B), jnp.bfloat16)
+
     send_p.wait_recv()
     other_p = pltpu.make_async_copy(pvm, psm.at[other], loc.at[3])
     other_p.start()
 
     for h in range(1, hops):
-        for q in range(CHUNKS):
+        for q in range(chunks):
             z_forward(0, q, h)
 
     local_h.wait()
@@ -146,22 +200,51 @@
     total = nb * R
 
     def index(half, i, s):
-        named = psm[half, i, s]
+        named = psm[half, s, i]
         if line:
             return named
         return lax.rem(named - (r - 2) * nb + total, total)
 
-    def product(win, i):
-        sums = None
+    def turn(i, _):
         for half in range(2):
             for s in range(half_nnz):
-                term = lax.dot_general(
-                    win[index(half, i, s)], hall[half, i, s], NT, preferred_element_type=jnp.float32
-                )
-                sums = term if sums is None else sums + term
-        return sums
-
-    for q in range(CHUNKS):
+                hall[half, i, s] = hall[half, i, s].T
+        return 0
+
+    lax.fori_loop(0, nb, turn, 0, unroll=2)
+
+    if ends:
+        @pl.when(from_end)
+        def _():
+            for j in range(2):
+                x_copy(j).start()
+
+    def product(win, i, held_back=False):
+        def place(half, s):
+            named = index(half, i, s)
+            if held_back and half == 1:
+                away = jnp.logical_and(outer, named // nb != r)
+                named = jnp.where(away, zero_block, named)
+            return named
+
+        picked = [win[place(half, s)] for half in range(2) for s in range(half_nnz)]
+        stored = [hall[half, i].reshape(half_nnz * B, B) for half in range(2)]
+        return jnp.dot(
+            jnp.concatenate(picked, axis=1), jnp.concatenate(stored, axis=0),
+            preferred_element_type=jnp.float32,
+        )
+
+    if ends:
+        @pl.when(inner)
+        def _():
+            def clear(i, _):
+                for q in range(chunks):
+                    s_in[q][i] = jnp.zeros((vc, B), jnp.bfloat16)
+                return 0
+
+            lax.fori_loop(0, nb, clear, 0)
+
+    for q in range(chunks):
         z_wait(0, q, hops - 1)
 
         def first_row(i, _, q=q):
@@ -172,9 +255,53 @@
         lax.fori_loop(0, nb, first_row, 0, unroll=UNROLL)
         z_start(1, q, 0)
 
-    for h in range(1, hops):
-        for q in range(CHUNKS):
+    hops2 = hops - 1 if ends else hops
+    for h in range(1, hops2):
+        for q in range(chunks):
             z_forward(1, q, h)
+
+    if ends:
+        @pl.when(inner)
+        def _():
+            px_copy(0).wait_recv()
+            names = pltpu.make_async_copy(pxv, pxs, loc.at[4 + chunks])
+            names.start()
+            names.wait()
+
+        @pl.when(relay)
+        def _():
+            for j in range(2):
+                x_copy(j).wait_recv()
+                y_copy(j).start()
+            for j in range(2):
+                y_copy(j).wait_send()
+
+        @pl.when(relayed)
+        def _():
+            for j in range(2):
+                y_copy(j).wait_recv()
+
+        @pl.when(inner)
+        def _():
+            def turn_x(i, _):
+                for s in range(half_nnz):
+                    hx[i, s] = hx[i, s].T
+                return 0
+
+            lax.fori_loop(0, nb, turn_x, 0, unroll=2)
+
+        def s_copy(q):
+            return pltpu.make_async_remote_copy(
+                s_out[q], s_in[q], s_send.at[q], s_recv.at[q],
+                device_id=(k, mate, c, p), device_id_type=MESH,
+            )
+
+        def e_copy(q, which):
+            block = pl.ds((edge_near, edge_far)[which], 1)
+            return pltpu.make_async_remote_copy(
+                win2[q].at[block], win2[q].at[block], e_send.at[q, which], e_recv.at[q, which],
+                device_id=(k, mate, c, p), device_id_type=MESH,
+            )
 
     def group(j):
         o = lax.rem(g + j, G)
@@ -184,13 +311,41 @@
         return pl.ds(pl.multiple_of(gi * V + q * vc, vc), vc)
 
     tail = []
-    for q in range(CHUNKS):
-        z_wait(1, q, hops - 1)
+    for q in range(chunks):
+        z_wait(1, q, hops2 - 1)
+        if ends:
+            @pl.when(inner)
+            def _(q=q):
+                for which in range(2):
+                    e_copy(q, which).start()
+
+                def end_row(i, _):
+                    picked = []
+                    for s in range(half_nnz):
+                        named = pxs[s, i]
+                        picked.append(win2[q][jnp.where(named // nb == end, zero_block, named)])
+                    s_out[q][i] = jnp.dot(
+                        jnp.concatenate(picked, axis=1), hx[i].reshape(half_nnz * B, B),
+                        preferred_element_type=jnp.float32,
+                    ).astype(jnp.bfloat16)
+                    return 0
+
+                lax.fori_loop(0, nb, end_row, 0, unroll=UNROLL)
+                s_copy(q).start()
+
+            @pl.when(outer)
+            def _(q=q):
+                for which in range(2):
+                    e_copy(q, which).wait_recv()
+                s_copy(q).wait_recv()
 
         def filtered_row(i, _, q=q):
             first = win2[q][own + i].astype(jnp.float32)
             start = win1[q][own + i].astype(jnp.float32)
-            value = 2.0 * ((product(win2[q], i) - centre * first) * inverse) - start
+            sums = product(win2[q], i, ends)
+            if ends:
+                sums = sums + s_in[q][i].astype(jnp.float32)
+            value = 2.0 * ((sums - centre * first) * inverse) - start
             filt[pl.ds(q * vc, vc), pl.ds(pl.multiple_of(i * B, B), B)] = value.astype(jnp.bfloat16)
             return 0
 
@@ -215,7 +370,7 @@
         copy.start()
         tail.append(copy)
 
-    for q in range(CHUNKS):
+    for q in range(chunks):
         for j in range(1, G):
             source = lax.rem(g - j + G, G)
             pltpu.make_async_remote_copy(
@@ -277,10 +432,23 @@
     gram_ref[...] = gram * (1.0 / (total * B))
 
     for step in range(2):
-        for q in range(CHUNKS):
+        for q in range(chunks):
             for h in range(hops):
                 for way in range(2):
-                    when(sends(way, h), lambda a=(step, q, way, h): z_copy(*a).wait_send())
+                    when(sends(step, way, h), lambda a=(step, q, way, h): z_copy(*a).wait_send())
+    if ends:
+        @pl.when(from_end)
+        def _():
+            for j in range(2):
+                px_copy(j).wait_send()
+                x_copy(j).wait_send()
+
+        @pl.when(inner)
+        def _():
+            for q in range(chunks):
+                s_copy(q).wait_send()
+                for which in range(2):
+                    e_copy(q, which).wait_send()
     send_p.wait_send()
     send_h.wait_send()
     for copy in tail:
@@ -288,7 +456,7 @@
     for j in range(R // 2):
         for q in range(2):
             pl.when(b_elsewhere(j, q))(lambda j=j, q=q: b_copy(j, q).wait_send())
-    for q in range(CHUNKS):
+    for q in range(chunks):
         rows = pl.ds(pl.multiple_of(p * V + q * vc, vc), vc)
         pltpu.make_async_copy(filt.at[pl.ds(q * vc, vc)], out_ref.at[rows], loc.at[4 + q]).wait()
         theirs = pl.ds(pl.multiple_of(other * V + q * vc, vc), vc)
@@ -305,7 +473,8 @@
     hops = R - 1 if line else 2
     slots = R if line else 5
     V = per_dev // 2
-    vc = V // CHUNKS
+    chunks = 4 if V % 64 == 0 else max(V // 16, 1)
+    vc = V // chunks
     G = 2 * C
     K = per_dev * C
     bw = local_rows // G
@@ -313,8 +482,18 @@
     b_type = jnp.bfloat16 if rt % 16 == 0 else jnp.float32
     bf16 = jnp.bfloat16
     dma = pltpu.SemaphoreType.DMA
+    end_scratch = []
+    if R == 4:
+        end_scratch = [
+            pltpu.VMEM((nb, half_nnz, B, B), bf16),
+            pltpu.VMEM((half_nnz, nb), jnp.int32),
+            pltpu.SMEM((half_nnz, nb), jnp.int32),
+        ] + [pltpu.VMEM((nb, vc, B), bf16)] * (2 * chunks) + [
+            dma((2,)), dma((2,)), dma((2,)), dma((2,)), dma((2,)), dma,
+            dma((chunks,)), dma((chunks,)), dma((chunks, 2)), dma((chunks, 2)),
+        ]
     return pl.pallas_call(
-        functools.partial(kernel, R, C, hops, line),
+        functools.partial(kernel, R, C, hops, line, chunks),
         out_shape=(
             jax.ShapeDtypeStruct((per_dev, local_rows), bf16),
             jax.ShapeDtypeStruct((rt, ct), jnp.float32),
@@ -328,8 +507,8 @@
         out_specs=(pl.BlockSpec(memory_space=pl.ANY), pl.BlockSpec(memory_space=pltpu.VMEM)),
         scratch_shapes=[
             pltpu.VMEM((2, nb, half_nnz, B, B), bf16),
-            pltpu.VMEM((nb, half_nnz), jnp.int32),
-            pltpu.SMEM((2, nb, half_nnz), jnp.int32),
+            pltpu.VMEM((half_nnz, nb), jnp.int32),
+            pltpu.SMEM((2, half_nnz, nb), jnp.int32),
             pltpu.VMEM((V, local_rows), bf16),
             pltpu.VMEM((V, local_rows), bf16),
             pltpu.VMEM((K, bw), bf16),
@@ -338,19 +517,20 @@
             pltpu.VMEM((R // 2, rt, ct), b_type),
             pltpu.VMEM((R, rt, ct), b_type),
         ]
-        + [pltpu.VMEM((slots * nb, vc, B), bf16)] * (2 * CHUNKS)
+        + [pltpu.VMEM((slots * nb + 1, vc, B), bf16)] * (2 * chunks)
         + [
-            dma((2, CHUNKS, 2, hops)), dma((2, CHUNKS, 2, hops)),
-            dma, dma, dma, dma, dma((4 + CHUNKS,)),
-            dma((CHUNKS,)), dma((CHUNKS,)),
-            dma((CHUNKS, G)), dma((CHUNKS, G)),
+            dma((2, chunks, 2, hops)), dma((2, chunks, 2, hops)),
+            dma, dma, dma, dma, dma((5 + chunks,)),
+            dma((chunks,)), dma((chunks,)),
+            dma((chunks, G)), dma((chunks, G)),
             dma((G,)), dma((G,)),
             dma((R // 2, 2)), dma((R,)),
-        ],
+        ]
+        + end_scratch,
         compiler_params=pltpu.CompilerParams(
-            collective_id=0, has_side_effects=True, vmem_limit_bytes=40 * 1024 * 1024
+            collective_id=0, has_side_effects=True, vmem_limit_bytes=60 * 1024 * 1024
         ),
-    )(hamiltonian, pattern, vectors, spectrum)
+    )(hamiltonian, pattern.T, vectors, spectrum)
 
 
 def solution(mesh):

time: 97.6 us -> 119 us (1.22)
  Pallas kernels: 90.6 us -> 115 us
  local copies, waits for them, and re-layouts: 6.12 us -> 3.66 us
    pallas_call x1, Pallas kernels: 90.6 us -> 115 us  [on_device(): pl.pallas_call(functools.partial(kernel, R, C, hops, line, chunks), out_s...]
    unnamed x9 -> x2, local copies, waits for them, and re-layouts: 6.12 us -> 3.66 us
where the time goes in v2:
time: 119 us
  Pallas kernels  115 us (97%)
  local copies, waits for them, and re-layouts  3.66 us (3%)
    pallas_call x1, Pallas kernels, on_device(): pl.pallas_call(functools.partial(kernel, R, C, hops, line, chunks), out_s...  115 us
    unnamed x2, local copies, waits for them, and re-layouts  3.66 us

profile of v2, /device:TPU:0, one launch (start us, length us, event | category | flops | bytes accessed | tf_op | source)
XLA Modules:
  0.0 119.2 jit_solution(4894853923205964882)
XLA Ops:
  0.6 114.9 %shard_map.59 = (bf16[128,4096]{1,0:T(8,128)(2,1)}, f32[64,128]{1,0:T(8,128)}) custom-call(bf16[32,3,128,128]{3,2,1,0:T(8,128)(2,1)} %h_ref.1, s32[3,32]{1,0:T(4,128)} %bitcast.1, bf16[128,4096]{1,0:T(8,128)(2,1)} %vec_ref.1, f32[2]{0:T(128)} %spec_ref.1), custom_call_target="tpu_custom_call" | custom-call | tf_op jit(solution)/shard_map/pallas_call | solution.py:495
  115.5 2.3 %copy.8 = bf16[128,4096]{1,0:T(8,128)(2,1)} copy(bf16[128,4096]{1,0:T(8,128)(2,1)} %get-tuple-element.4) | data formatting | bytes 2097152
  117.8 1.4 %copy.9 = f32[64,128]{1,0:T(8,128)} copy(f32[64,128]{1,0:T(8,128)} %get-tuple-element.5) | data formatting | bytes 65536

commit v3 on v2

--- a/solution.py
+++ b/solution.py
@@ -26,7 +26,7 @@
     if ends:
         hx, pxv, pxs = extra[:3]
         s_out, s_in = extra[3:3 + chunks], extra[3 + chunks:3 + 2 * chunks]
-        x_send, x_recv, y_send, y_recv, px_send, px_recv, s_send, s_recv, e_send, e_recv = extra[3 + 2 * chunks:]
+        x_send, x_recv, w_send, w_recv, y_send, y_recv, px_send, px_recv, s_send, s_recv, e_send, e_recv = extra[3 + 2 * chunks:]
     k, r, c, p = (lax.axis_index(n) for n in ("kpt", "row", "col", "rep"))
     G = 2 * C
     g = c * 2 + p
@@ -149,19 +149,27 @@
     send_h.start()
     arrive_h = pltpu.make_async_remote_copy(h_ref, hall.at[other], h_send, h_recv, device_id=partner, device_id_type=MESH)
     if ends:
-        piece = nb // 2
+        pieces = 4
+        piece = nb // (2 * pieces)
+
+        def rows_of(half, j):
+            return pl.ds((half * pieces + j) * piece, piece)
 
         def x_copy(j):
-            part_rows = pl.ds(j * piece, piece)
             return pltpu.make_async_remote_copy(
-                h_ref.at[part_rows], hx.at[part_rows], x_send.at[j], x_recv.at[j],
+                h_ref.at[rows_of(c, j)], hx.at[rows_of(c, j)], x_send.at[j], x_recv.at[j],
                 device_id=(k, mate, c, p), device_id_type=MESH,
             )
 
-        def y_copy(j):
-            part_rows = pl.ds(j * piece, piece)
+        def w_copy(half, j):
             return pltpu.make_async_remote_copy(
-                hx.at[part_rows], hx.at[part_rows], y_send.at[j], y_recv.at[j],
+                hx.at[rows_of(half, j)], hx.at[rows_of(half, j)], w_send.at[j], w_recv.at[j],
+                device_id=(k, r, 1 - c, p), device_id_type=MESH,
+            )
+
+        def y_copy(half, n, j):
+            return pltpu.make_async_remote_copy(
+                hx.at[rows_of(half, j)], hx.at[rows_of(half, j)], y_send.at[n, j], y_recv.at[n, j],
                 device_id=partner, device_id_type=MESH,
             )
 
@@ -178,6 +186,8 @@
         def _():
             for q in range(2):
                 px_copy(q).start()
+            for j in range(pieces):
+                x_copy(j).start()
 
         for q in range(chunks):
             win2[q][zero_block] = jnp.zeros((vc, B), jnp.bfloat16)
@@ -212,12 +222,6 @@
         return 0
 
     lax.fori_loop(0, nb, turn, 0, unroll=2)
-
-    if ends:
-        @pl.when(from_end)
-        def _():
-            for j in range(2):
-                x_copy(j).start()
 
     def product(win, i, held_back=False):
         def place(half, s):
@@ -235,6 +239,14 @@
         )
 
     if ends:
+        @pl.when(relay)
+        def _():
+            for j in range(pieces):
+                x_copy(j).wait_recv()
+                w_copy(c, j).start()
+                y_copy(c, 0, j).start()
+
+    if ends:
         @pl.when(inner)
         def _():
             def clear(i, _):
@@ -255,11 +267,6 @@
         lax.fori_loop(0, nb, first_row, 0, unroll=UNROLL)
         z_start(1, q, 0)
 
-    hops2 = hops - 1 if ends else hops
-    for h in range(1, hops2):
-        for q in range(chunks):
-            z_forward(1, q, h)
-
     if ends:
         @pl.when(inner)
         def _():
@@ -270,16 +277,19 @@
 
         @pl.when(relay)
         def _():
-            for j in range(2):
-                x_copy(j).wait_recv()
-                y_copy(j).start()
-            for j in range(2):
-                y_copy(j).wait_send()
+            for j in range(pieces):
+                w_copy(1 - c, j).wait_recv()
+                y_copy(1 - c, 1, j).start()
+            for j in range(pieces):
+                w_copy(c, j).wait_send()
+                y_copy(c, 0, j).wait_send()
+                y_copy(1 - c, 1, j).wait_send()
 
         @pl.when(relayed)
         def _():
-            for j in range(2):
-                y_copy(j).wait_recv()
+            for j in range(pieces):
+                y_copy(c, 0, j).wait_recv()
+                y_copy(1 - c, 1, j).wait_recv()
 
         @pl.when(inner)
         def _():
@@ -302,6 +312,11 @@
                 win2[q].at[block], win2[q].at[block], e_send.at[q, which], e_recv.at[q, which],
                 device_id=(k, mate, c, p), device_id_type=MESH,
             )
+
+    hops2 = hops - 1 if ends else hops
+    for h in range(1, hops2):
+        for q in range(chunks):
+            z_forward(1, q, h)
 
     def group(j):
         o = lax.rem(g + j, G)
@@ -441,6 +456,7 @@
         def _():
             for j in range(2):
                 px_copy(j).wait_send()
+            for j in range(pieces):
                 x_copy(j).wait_send()
 
         @pl.when(inner)
@@ -483,13 +499,13 @@
     bf16 = jnp.bfloat16
     dma = pltpu.SemaphoreType.DMA
     end_scratch = []
-    if R == 4:
+    if R == 4 and C == 2:
         end_scratch = [
             pltpu.VMEM((nb, half_nnz, B, B), bf16),
             pltpu.VMEM((half_nnz, nb), jnp.int32),
             pltpu.SMEM((half_nnz, nb), jnp.int32),
         ] + [pltpu.VMEM((nb, vc, B), bf16)] * (2 * chunks) + [
-            dma((2,)), dma((2,)), dma((2,)), dma((2,)), dma((2,)), dma,
+            dma((4,)), dma((4,)), dma((4,)), dma((4,)), dma((2, 4)), dma((2, 4)), dma((2,)), dma,
             dma((chunks,)), dma((chunks,)), dma((chunks, 2)), dma((chunks, 2)),
         ]
     return pl.pallas_call(

time: 119 us -> 91.6 us (0.77)
  Pallas kernels: 115 us -> 87.1 us
    pallas_call x1, Pallas kernels: 115 us -> 87.1 us  [on_device(): pl.pallas_call(functools.partial(kernel, R, C, hops, line, chunks), out_s...]
where the time goes in v3:
time: 91.6 us; the launch traced here: 91.4 us
  Pallas kernels  87.1 us (95%)
  local copies, waits for them, and re-layouts  3.66 us (4%)
    pallas_call x1, Pallas kernels, on_device(): pl.pallas_call(functools.partial(kernel, R, C, hops, line, chunks), out_s...  87.1 us
    unnamed x2, local copies, waits for them, and re-layouts  3.66 us

profile of v3, /device:TPU:0, one launch (start us, length us, event | category | flops | bytes accessed | tf_op | source)
XLA Modules:
  0.0 91.4 jit_solution(11776543001810513955)
XLA Ops:
  0.6 87.1 %shard_map.59 = (bf16[128,4096]{1,0:T(8,128)(2,1)}, f32[64,128]{1,0:T(8,128)}) custom-call(bf16[32,3,128,128]{3,2,1,0:T(8,128)(2,1)} %h_ref.1, s32[3,32]{1,0:T(4,128)} %bitcast.1, bf16[128,4096]{1,0:T(8,128)(2,1)} %vec_ref.1, f32[2]{0:T(128)} %spec_ref.1), custom_call_target="tpu_custom_call" | custom-call | tf_op jit(solution)/shard_map/pallas_call | solution.py:511
  87.7 2.3 %copy.8 = bf16[128,4096]{1,0:T(8,128)(2,1)} copy(bf16[128,4096]{1,0:T(8,128)(2,1)} %get-tuple-element.4) | data formatting | bytes 2097152
  90.0 1.4 %copy.9 = f32[64,128]{1,0:T(8,128)} copy(f32[64,128]{1,0:T(8,128)} %get-tuple-element.5) | data formatting | bytes 65536

commit v4 on v3

--- a/solution.py
+++ b/solution.py
@@ -239,14 +239,6 @@
         )
 
     if ends:
-        @pl.when(relay)
-        def _():
-            for j in range(pieces):
-                x_copy(j).wait_recv()
-                w_copy(c, j).start()
-                y_copy(c, 0, j).start()
-
-    if ends:
         @pl.when(inner)
         def _():
             def clear(i, _):
@@ -257,6 +249,14 @@
             lax.fori_loop(0, nb, clear, 0)
 
     for q in range(chunks):
+        if ends:
+            @pl.when(relay)
+            def _(q=q):
+                for j in range(q * pieces // chunks, (q + 1) * pieces // chunks):
+                    x_copy(j).wait_recv()
+                    w_copy(c, j).start()
+                    y_copy(c, 0, j).start()
+
         z_wait(0, q, hops - 1)
 
         def first_row(i, _, q=q):

time: 91.6 us -> 91.8 us (level)
  no operation moved by 1% of the time
where the time goes in v4:
time: 91.8 us; the launch traced here: 91.6 us
  Pallas kernels  87.3 us (95%)
  local copies, waits for them, and re-layouts  3.66 us (4%)
    pallas_call x1, Pallas kernels, on_device(): pl.pallas_call(functools.partial(kernel, R, C, hops, line, chunks), out_s...  87.3 us
    unnamed x2, local copies, waits for them, and re-layouts  3.66 us

profile of v4, /device:TPU:0, one launch (start us, length us, event | category | flops | bytes accessed | tf_op | source)
XLA Modules:
  0.0 91.6 jit_solution(2460494915524643037)
XLA Ops:
  0.6 87.3 %shard_map.59 = (bf16[128,4096]{1,0:T(8,128)(2,1)}, f32[64,128]{1,0:T(8,128)}) custom-call(bf16[32,3,128,128]{3,2,1,0:T(8,128)(2,1)} %h_ref.1, s32[3,32]{1,0:T(4,128)} %bitcast.1, bf16[128,4096]{1,0:T(8,128)(2,1)} %vec_ref.1, f32[2]{0:T(128)} %spec_ref.1), custom_call_target="tpu_custom_call" | custom-call | tf_op jit(solution)/shard_map/pallas_call | solution.py:511
  87.9 2.3 %copy.8 = bf16[128,4096]{1,0:T(8,128)(2,1)} copy(bf16[128,4096]{1,0:T(8,128)(2,1)} %get-tuple-element.4) | data formatting | bytes 2097152
  90.2 1.4 %copy.9 = f32[64,128]{1,0:T(8,128)} copy(f32[64,128]{1,0:T(8,128)} %get-tuple-element.5) | data formatting | bytes 65536
